TPU v7x, 512 devices: a whole 4x8x8 slice. The times are simulated.
512 devices in a mesh: seq: 32 (over y, x), head: 16 (over z, core).
Axes of the slice: x: 4, y: 8, z: 8, core: 2. Of those that a mesh axis runs over, the one named last changes fastest.
Arguments:
- queries: bfloat16 [2048, 8192], P('seq', 'head'), may hold values from -6 to 6
- keys: bfloat16 [2048, 1024], P('seq'), may hold values from -6 to 6
- values: bfloat16 [2048, 1024], P('seq'), may hold values from -6 to 6
- vertical: int32 [64, 8], replicated, may hold values from -1 to 31, as said below
- slash: int32 [64, 8], replicated, may hold values from -1 to 31, as said below
- plan: int32 [64], replicated, may hold values from 0 to 63, each once
Outputs:
- attended: bfloat16 [2048, 8192], P('seq', 'head')
Inputs may be any that keep to these rules, and one draw needn't show every extreme that they name: `vertical`: entries of 0 or more name key blocks of 64 positions; -1 marks an unused entry, and every row has at least one used entry. `slash`: entries of 0 or more are offsets back from a query's own block; -1 marks an unused entry; the first entry of every row is 0. `plan`: A permutation of the query heads.
All inputs are finite; a program needn't handle non-finite values.
Results may differ from a plain program's by a relative error of at most 0.0044.
Values may be sent and summed in bfloat16 or wider, within the bound.
A program may use at most 64 MiB of HBM per device.

v0:
```python
import jax
import jax.numpy as jnp
from jax import lax
from jax.sharding import PartitionSpec as P

HD = 128
QH = 64
KVH = 8
BLK = 64
floor_value = -1e30


def block_mask(query_blocks, key_blocks, vertical_rows, slash_rows, query_pos, key_pos):
    vertical_hit = jnp.any(vertical_rows[:, :, None] == key_blocks[None, None, :], axis=1)
    distance = query_blocks[:, None] - key_blocks[None, :]
    slash_hit = jnp.zeros((slash_rows.shape[0],) + distance.shape, jnp.bool_)
    for column in range(slash_rows.shape[1]):
        slash_hit = slash_hit | (slash_rows[:, column][:, None, None] == distance[None])
    causal = key_pos[None, :] <= query_pos[:, None]
    return causal[None] & (vertical_hit[:, None, :] | slash_hit)


def attend(carried, query_group, key_group, value_group, allowed, score_scale):
    max_old, totals_old, sums_old = carried
    scores = (
        jnp.einsum("qgh,kgh->gqk", query_group, key_group, preferred_element_type=jnp.float32)
        * score_scale
    )
    masked = jnp.where(allowed, scores, floor_value)
    max_new = jnp.maximum(max_old, jnp.max(masked, axis=2))
    weights = jnp.exp(masked - max_new[:, :, None])
    totals_new = jnp.sum(weights, axis=2)
    mixture = jnp.einsum(
        "gqk,kgh->qgh",
        weights.astype(jnp.bfloat16),
        value_group,
        preferred_element_type=jnp.float32,
    )
    return (max_new, totals_new, mixture)


def per_device(queries, keys, values, vertical, slash, plan):
    slot_count = plan.shape[0] // lax.axis_size("head")
    query_len = queries.shape[0]
    key_len = keys.shape[0]
    group_size = QH // KVH
    my_heads = lax.dynamic_slice_in_dim(plan, lax.axis_index("head") * slot_count, slot_count)
    kv_index = my_heads // group_size
    slot_column = jnp.arange(slot_count, dtype=jnp.int32)
    key_pick = jnp.take(keys.reshape(key_len, KVH, HD), kv_index, axis=1).reshape(
        key_len, slot_count * HD
    )
    value_pick = jnp.take(values.reshape(key_len, KVH, HD), kv_index, axis=1).reshape(
        key_len, slot_count * HD
    )
    gathered = lax.all_gather(queries, "head", axis=1, tiled=True)
    query_sel = jnp.take(gathered.reshape(query_len, QH, HD), my_heads, axis=1)
    vertical_sel = jnp.take(vertical, my_heads, axis=0)
    slash_sel = jnp.take(slash, my_heads, axis=0)
    query_pos = lax.axis_index("seq") * query_len + jnp.arange(query_len, dtype=jnp.int32)
    query_blocks = query_pos // BLK
    score_scale = HD ** (-0.5)

    def select_rows(rows):
        return jnp.take(rows.reshape(rows.shape[0], slot_count, HD), slot_column, axis=1)

    initial = (
        jnp.full((slot_count, query_len), floor_value, jnp.float32),
        jnp.zeros((slot_count, query_len), jnp.float32),
        jnp.zeros((query_len, slot_count, HD), jnp.float32),
    )
    key_piece = select_rows(lax.all_gather(key_pick, "seq", axis=0, tiled=True))
    value_piece = select_rows(lax.all_gather(value_pick, "seq", axis=0, tiled=True))
    piece_len = key_piece.shape[0]
    key_pos = jnp.arange(piece_len, dtype=jnp.int32)
    allowed = block_mask(query_blocks, key_pos // BLK, vertical_sel, slash_sel, query_pos, key_pos)
    max_parts = []
    total_parts = []
    sum_parts = []
    for lead in range(0, slot_count, 2):
        previous = (
            initial[0][lead : lead + 2],
            initial[1][lead : lead + 2],
            initial[2][:, lead : lead + 2],
        )
        updated = attend(
            previous,
            query_sel[:, lead : lead + 2],
            key_piece[:, lead : lead + 2],
            value_piece[:, lead : lead + 2],
            allowed[lead : lead + 2],
            score_scale,
        )
        max_parts.append(updated[0])
        total_parts.append(updated[1])
        sum_parts.append(updated[2])
    output = (
        jnp.concatenate(sum_parts, axis=1)
        / jnp.transpose(jnp.concatenate(total_parts, axis=0))[:, :, None]
    )
    return output.reshape(query_len, slot_count * HD).astype(jnp.bfloat16)


def solution(mesh):
    in_specs = (P("seq", "head"), P("seq", None), P("seq", None), P(), P(), P())
    out_specs = P("seq", "head")
    return jax.shard_map(
        per_device, mesh=mesh, in_specs=in_specs, out_specs=out_specs, check_vma=False
    )
```

profile of v0, /device:TPU:16, one launch (start us, length us, event | category | flops | bytes accessed | tf_op | source)
XLA Modules:
  0.0 250.0 jit_solution(17985091205724103392)
XLA Ops:
  6.5 0.0 copy-start
  6.5 0.0 all-gather.6.cloned.1.call-start
  6.5 0.7 all-gather.6.cloned.1.call-update
  7.3 0.0 all-gather.4.cloned.1.call-start
  7.3 0.7 compare_and_fusion
  8.1 0.0 copy-done
  8.1 0.6 gather_fusion.5
  8.7 0.9 copy_bitcast_fusion.1
  9.6 0.6 gather_fusion.1
  10.2 0.1 select_bitcast_fusion.3
  10.3 0.6 copy.48
  10.9 0.0 all-gather.4.cloned.1.call-update
  10.9 0.0 all-gather.8.cloned.1.call-start
  11.0 0.6 copy.49
  11.6 0.0 all-gather.8.cloned.1.call-update
  11.7 0.8 copy.28
  12.4 0.8 copy.29
  13.2 0.6 gather_fusion.3
  13.8 0.6 gather_fusion.4
  14.4 0.1 broadcast_select_fusion.4
  14.5 0.3 slice_reduce_fusion.7
  14.8 0.2 compare_reduce_fusion
  14.9 0.1 iota_compare_fusion
  15.1 0.1 broadcast_subtract_fusion
  15.2 2.2 or_and_fusion
  17.4 38.6 %all-gather.6.cloned.1.call-done = bf16[64,8192]{1,0:T(8,128)(2,1)} async-done(((bf16[64,512]{1,0:T(8,128)(2,1)}), bf16[64,8192]{1,0:T(8,128)(2,1)}) %all-gather.6.cloned.1.call-update) | async-done | bytes 1048592 | tf_op jit(solution)/shard_map/all_gather | solution.py:56
  56.0 1.5 copy_bitcast_fusion
  57.5 0.6 gather_fusion
  58.1 82.0 %all-gather.4.cloned.1.call-done = bf16[2048,512]{1,0:T(8,128)(2,1)} async-done(((bf16[64,512]{1,0:T(8,128)(2,1)}), bf16[2048,512]{1,0:T(8,128)(2,1)}) %all-gather.4.cloned.1.call-update) | async-done | bytes 2097168 | tf_op jit(solution)/shard_map/all_gather | solution.py:73
  140.1 3.9 %copy.26 = bf16[2048,512]{0,1:T(8,128)(2,1)} copy(bf16[2048,512]{1,0:T(8,128)(2,1)} %all-gather.4.cloned.1.call-done) | data formatting | bytes 4194304 | tf_op jit(solution)/shard_map/all_gather | solution.py:73
  144.1 3.0 %copy.27 = bf16[2048,4,128]{2,0,1:T(8,128)(2,1)S(1)} copy(bf16[2048,4,128]{0,2,1:T(8,128)(2,1)} %bitcast.53) | data formatting | bytes 4194304 | tf_op jit(solution)/shard_map/reshape | solution.py:65
  147.1 76.9 %all-gather.8.cloned.1.call-done = bf16[2048,512]{1,0:T(8,128)(2,1)} async-done(((bf16[64,512]{1,0:T(8,128)(2,1)}), bf16[2048,512]{1,0:T(8,128)(2,1)}) %all-gather.8.cloned.1.call-update) | async-done | bytes 2097168 | tf_op jit(solution)/shard_map/all_gather | solution.py:72
  224.1 4.0 %copy.33 = bf16[2048,512]{0,1:T(8,128)(2,1)} copy(bf16[2048,512]{1,0:T(8,128)(2,1)} %all-gather.8.cloned.1.call-done) | data formatting | bytes 4194304 | tf_op jit(solution)/shard_map/all_gather | solution.py:72
  228.0 4.0 %copy.34 = bf16[2048,4,128]{2,0,1:T(8,128)(2,1)} copy(bf16[2048,4,128]{0,2,1:T(8,128)(2,1)} %bitcast.54) | data formatting | bytes 4194304 | tf_op jit(solution)/shard_map/reshape | solution.py:65
  232.0 2.1 gather_fusion.2
  234.1 0.0 copy-start.1
  234.1 3.9 %gather_fusion.6 = bf16[4,2048,128]{2,1,0:T(8,128)(2,1)} fusion(bf16[2048,4,128]{2,0,1:T(8,128)(2,1)} %copy.34, s32[1024]{0:T(1024)S(1)} %pad_clamp_fusion), kind=kCustom, calls=%fused_computation.4.clone | custom fusion | bytes 4194320 | tf_op jit(solution)/shard_map/jit(_take)/gather | solution.py:65
  238.0 0.0 copy-done.1
  238.0 2.0 select_bitcast_fusion.1
  240.0 0.6 fusion.23
  240.7 0.7 fusion.24
  241.3 0.3 fusion.8
  241.6 0.4 convolution_bitcast_fusion
  242.0 0.4 convolution_bitcast_fusion.1
  242.4 0.3 fusion.6
  242.8 0.7 copy_bitcast_fusion.3
  (11 shorter events, 0.1 us)
Async XLA Ops:
  6.5 1.5 copy-start
  6.5 49.5 %all-gather.6.cloned.1.call-start = ((), (), s32[]{:S(2)}) async-start(), calls=%async_computation.1 | async-start | bytes 1114112 | tf_op jit(solution)/shard_map/all_gather | solution.py:56
  7.3 132.9 %all-gather.4.cloned.1.call-start = ((), (), s32[]{:S(2)}) async-start(), calls=%async_computation | async-start | bytes 2162688 | tf_op jit(solution)/shard_map/all_gather | solution.py:73
  10.9 213.1 %all-gather.8.cloned.1.call-start = ((), (), s32[]{:S(2)}) async-start(), calls=%async_computation.2 | async-start | bytes 2162688 | tf_op jit(solution)/shard_map/all_gather | solution.py:72
  234.1 3.9 %copy-start.1 = (bf16[4,2048,128]{2,1,0:T(8,128)(2,1)S(1)}, bf16[4,2048,128]{2,1,0:T(8,128)(2,1)}, u32[]{:S(2)}) copy-start(bf16[4,2048,128]{2,1,0:T(8,128)(2,1)} %gather_fusion.2) | copy-start | bytes 6291460
Sparse Core Ops, SparseCore 0:
  9.5 46.4 all-gather.5
  59.2 80.8 all-gather.3
  143.3 80.7 all-gather.7
where the time goes:
time: 251 us; the launch traced here: 250 us
  waiting for transfers between devices  198 us (79%)
  local copies, waits for them, and re-layouts  29.3 us (12%)
  between operations  13.3 us (5%)
  other arithmetic  6.95 us (3%)
    all_gather x1, waiting for transfers between devices, per_device(): lax.all_gather(value_pick, 'seq', axis=0, tiled=True)  82 us
    all_gather x1, waiting for transfers between devices, per_device(): key_piece = select_rows(lax.all_gather(key_pick, 'seq', axis=0, tiled=True))  76.9 us
    all_gather x1, waiting for transfers between devices, per_device(): gathered = lax.all_gather(queries, 'head', axis=1, tiled=True)  38.6 us
    reshape x2, local copies, waits for them, and re-layouts, select_rows(): rows.reshape(rows.shape[0], slot_count, HD)  6.99 us
    gather x2, local copies, waits for them, and re-layouts, select_rows(): jnp.take(rows.reshape(rows.shape[0], slot_count, HD), slot_column, axis=1)  5.99 us
  transfers between devices with their start and end apart: 3, of which 3 were waited for; matrix products, arithmetic and copies ran while one was open for 8% of the time, Pallas kernels for 0%

commit v1 on v0

--- a/solution.py
+++ b/solution.py
@@ -1,13 +1,43 @@
+import functools
 import jax
 import jax.numpy as jnp
 from jax import lax
 from jax.sharding import PartitionSpec as P
+from jax.lax import axis_index, axis_size, ppermute
 
 HD = 128
 QH = 64
 KVH = 8
 BLK = 64
 floor_value = -1e30
+
+
+def tell_the_hubs(sheet, array_dim):
+    reply = list(sheet.shape[1:])
+    reply[array_dim] *= sheet.shape[0]
+    return jnp.moveaxis(sheet, 0, array_dim).reshape(reply)
+
+
+def skins_test(v0, bus_axis):
+    x_next = axis_size(bus_axis)
+    local_next = axis_index(bus_axis)
+    piece_now, local_now = (x_next, local_next)
+    a_next, x_now = (v0[None], 1)
+    while x_now < piece_now:
+        e_now = ppermute(
+            a_next, axis_name=bus_axis, perm=[(d, d ^ x_now) for d in range(piece_now)]
+        )
+        low = local_now & x_now == 0
+        a_next = jnp.concatenate([jnp.where(low, a_next, e_now), jnp.where(low, e_now, a_next)])
+        x_now *= 2
+    return a_next
+
+
+def _touch_slices(mat, packet, axis_no):
+    return tell_the_hubs(skins_test(mat, packet), axis_no)
+
+
+notes_change = functools.partial(_touch_slices, packet="seq", axis_no=0)
 
 
 def block_mask(query_blocks, key_blocks, vertical_rows, slash_rows, query_pos, key_pos):
@@ -69,7 +99,7 @@
         jnp.zeros((slot_count, query_len), jnp.float32),
         jnp.zeros((query_len, slot_count, HD), jnp.float32),
     )
-    key_piece = select_rows(lax.all_gather(key_pick, "seq", axis=0, tiled=True))
+    key_piece = select_rows(notes_change(key_pick))
     value_piece = select_rows(lax.all_gather(value_pick, "seq", axis=0, tiled=True))
     piece_len = key_piece.shape[0]
     key_pos = jnp.arange(piece_len, dtype=jnp.int32)

time: 251 us -> 181 us (0.72)
  waiting for transfers between devices: 198 us -> 106 us
  starting transfers between devices: 0.08 us -> 27.6 us
  local copies, waits for them, and re-layouts: 29.3 us -> 21.6 us
  other arithmetic: 6.95 us -> 9.83 us
    all_gather x1 -> x0, waiting for transfers between devices: 76.9 us -> none  [per_device(): key_piece = select_rows(lax.all_gather(key_pick, 'seq', axis=0, tiled=True))]
    ppermute x0 -> x5, waiting for transfers between devices: none -> 57.8 us  [skins_test(): ppermute(a_next, axis_name=bus_axis, perm=[(d, d ^ x_now) for d in range(...]
    all_gather x1, waiting for transfers between devices: 38.6 us -> 0.01 us  [per_device(): gathered = lax.all_gather(queries, 'head', axis=1, tiled=True)]
    all_gather x1, waiting for transfers between devices: 82 us -> 47.5 us  [per_device(): lax.all_gather(value_pick, 'seq', axis=0, tiled=True)]
    ppermute x0 -> x5, starting transfers between devices: none -> 27.6 us  [skins_test(): ppermute(a_next, axis_name=bus_axis, perm=[(d, d ^ x_now) for d in range(...]
    all_gather x1 -> x0, local copies, waits for them, and re-layouts: 3.97 us -> none  [per_device(): key_piece = select_rows(lax.all_gather(key_pick, 'seq', axis=0, tiled=True))]
    reshape x2 -> x1, local copies, waits for them, and re-layouts: 6.99 us -> 3.03 us  [select_rows(): rows.reshape(rows.shape[0], slot_count, HD)]
    another operation x0 -> x3, local copies, waits for them, and re-layouts: none -> 3.96 us  [the longest x2 3.93 us: select_rows(): rows.reshape(rows.shape[0], slot_count, HD)]
  transfers between devices with their start and end apart: 3 -> 7, of which waited for: 3 -> 6; matrix products, arithmetic and copies ran while one was open for 8% -> 10% of each run, Pallas kernels for 0% -> 0%
where the time goes in v1:
time: 181 us
  waiting for transfers between devices  106 us (59%)
  starting transfers between devices  27.6 us (15%)
  local copies, waits for them, and re-layouts  21.6 us (12%)
  between operations  13.7 us (8%)
  other arithmetic  9.83 us (5%)
  matrix products  2.08 us (1%)
    ppermute x5, waiting for transfers between devices, skins_test(): ppermute(a_next, axis_name=bus_axis, perm=[(d, d ^ x_now) for d in range(...  57.8 us
    all_gather x1, waiting for transfers between devices, per_device(): lax.all_gather(value_pick, 'seq', axis=0, tiled=True)  47.5 us
    ppermute x5, starting transfers between devices, skins_test(): ppermute(a_next, axis_name=bus_axis, perm=[(d, d ^ x_now) for d in range(...  27.6 us
    gather x2, local copies, waits for them, and re-layouts, select_rows(): jnp.take(rows.reshape(rows.shape[0], slot_count, HD), slot_column, axis=1)  4.28 us
    all_gather x1, local copies, waits for them, and re-layouts, per_device(): lax.all_gather(value_pick, 'seq', axis=0, tiled=True)  3.94 us
    another operation x2, local copies, waits for them, and re-layouts, select_rows(): rows.reshape(rows.shape[0], slot_count, HD)  3.93 us
  transfers between devices with their start and end apart: 7, of which 6 were waited for; matrix products, arithmetic and copies ran while one was open for 10% of the time, Pallas kernels for 0%

profile of v1, /device:TPU:16, one launch (start us, length us, event | category | flops | bytes accessed | tf_op | source)
XLA Modules:
  0.0 180.9 jit_solution(9348073325339976916)
XLA Ops:
  6.5 0.0 copy-start
  6.5 0.0 copy-start.2
  6.5 0.0 copy-start.3
  6.5 0.0 all-gather.5.cloned.1.call-start
  6.5 0.7 all-gather.5.cloned.1.call-update
  7.3 0.0 all-gather.3.cloned.1.call-start
  7.3 0.7 compare_and_fusion
  8.1 0.0 copy-done
  8.1 0.6 gather_fusion.1
  8.7 0.9 copy_bitcast_fusion.2
  9.6 0.6 gather_fusion.5
  10.2 0.1 select_bitcast_fusion.3
  10.3 0.1 copy.31
  10.4 3.4 %collective-permute-start = (bf16[1,64,512]{2,1,0:T(8,128)(2,1)S(1)}, bf16[1,64,512]{2,1,0:T(8,128)(2,1)S(1)}, u32[]{:S(2)}, u32[]{:S(2)}) collective-permute-start(bf16[1,64,512]{2,1,0:T(8,128)(2,1)S(1)} %broadcast_in_dim_reshape.3), channel_id=1, source_target_pairs={{0,16},{16,0},{32,48},{48,32},{64,80},{80,64},{96,112},{112,96},{1... | collective-permute-start | bytes 196616 | tf_op jit(solution)/shard_map/ppermute | solution.py:27
  13.8 0.6 copy.44
  14.4 0.0 all-gather.3.cloned.1.call-update
  14.5 2.1 %collective-permute-done = bf16[1,64,512]{2,1,0:T(8,128)(2,1)S(1)} collective-permute-done((bf16[1,64,512]{2,1,0:T(8,128)(2,1)S(1)}, bf16[1,64,512]{2,1,0:T(8,128)(2,1)S(1)}, u32[]{:S(2)}, u32[]{:S(2)}) %collective-permute-start) | collective-permute-done | bytes 65568 | tf_op jit(solution)/shard_map/ppermute | solution.py:27
  16.6 4.9 %collective-permute-start.1 = (bf16[2,64,512]{2,1,0:T(8,128)(2,1)S(1)}, bf16[2,64,512]{2,1,0:T(8,128)(2,1)S(1)}, u32[]{:S(2)}, u32[]{:S(2)}) collective-permute-start(bf16[2,64,512]{2,1,0:T(8,128)(2,1)S(1)} %pad_maximum_fusion.4), channel_id=1, source_target_pairs={{0,32},{16,48},{32,0},{48,16},{64,96},{80,112},{96,64},{112,80},{1... | collective-permute-start | bytes 393224 | tf_op jit(solution)/shard_map/ppermute | solution.py:27
  21.5 0.1 iota_compare_fusion
  21.7 3.3 %collective-permute-done.1 = bf16[2,64,512]{2,1,0:T(8,128)(2,1)S(1)} collective-permute-done((bf16[2,64,512]{2,1,0:T(8,128)(2,1)S(1)}, bf16[2,64,512]{2,1,0:T(8,128)(2,1)S(1)}, u32[]{:S(2)}, u32[]{:S(2)}) %collective-permute-start.1) | collective-permute-done | bytes 131104 | tf_op jit(solution)/shard_map/ppermute | solution.py:27
  25.0 3.5 %collective-permute-start.2 = (bf16[4,64,512]{2,1,0:T(8,128)(2,1)S(1)}, bf16[4,64,512]{2,1,0:T(8,128)(2,1)S(1)}, u32[]{:S(2)}, u32[]{:S(2)}) collective-permute-start(bf16[4,64,512]{2,1,0:T(8,128)(2,1)S(1)} %pad_maximum_fusion.3), channel_id=1, source_target_pairs={{0,64},{16,80},{32,96},{48,112},{64,0},{80,16},{96,32},{112,48},{1... | collective-permute-start | bytes 786440 | tf_op jit(solution)/shard_map/ppermute | solution.py:27
  28.5 0.0 copy-done.2
  28.5 0.1 copy.27
  28.6 0.0 copy-done.3
  28.6 0.1 copy.28
  28.7 0.6 gather_fusion.3
  29.3 0.6 gather_fusion.4
  29.8 0.1 broadcast_select_fusion.14
  29.9 3.4 %collective-permute-done.2 = bf16[4,64,512]{2,1,0:T(8,128)(2,1)S(1)} collective-permute-done((bf16[4,64,512]{2,1,0:T(8,128)(2,1)S(1)}, bf16[4,64,512]{2,1,0:T(8,128)(2,1)S(1)}, u32[]{:S(2)}, u32[]{:S(2)}) %collective-permute-start.2) | collective-permute-done | bytes 262176 | tf_op jit(solution)/shard_map/ppermute | solution.py:27
  33.4 8.2 %collective-permute-start.3 = (bf16[8,64,512]{2,1,0:T(8,128)(2,1)S(1)}, bf16[8,64,512]{2,1,0:T(8,128)(2,1)S(1)}, u32[]{:S(2)}, u32[]{:S(2)}) collective-permute-start(bf16[8,64,512]{2,1,0:T(8,128)(2,1)S(1)} %pad_maximum_fusion.2), channel_id=1, source_target_pairs={{0,128},{16,144},{32,160},{48,176},{64,192},{80,208},{96,224},{112... | collective-permute-start | bytes 1572872 | tf_op jit(solution)/shard_map/ppermute | solution.py:27
  41.6 0.1 broadcast_subtract_fusion
  41.7 13.0 %collective-permute-done.3 = bf16[8,64,512]{2,1,0:T(8,128)(2,1)S(1)} collective-permute-done((bf16[8,64,512]{2,1,0:T(8,128)(2,1)S(1)}, bf16[8,64,512]{2,1,0:T(8,128)(2,1)S(1)}, u32[]{:S(2)}, u32[]{:S(2)}) %collective-permute-start.3) | collective-permute-done | bytes 524320 | tf_op jit(solution)/shard_map/ppermute | solution.py:27
  54.7 0.1 broadcast_select_fusion.3
  54.8 1.1 pad_maximum_fusion.1
  55.8 7.6 %collective-permute-start.4 = (bf16[16,64,512]{2,1,0:T(8,128)(2,1)}, bf16[16,64,512]{2,1,0:T(8,128)(2,1)S(1)}, u32[]{:S(2)}, u32[]{:S(2)}) collective-permute-start(bf16[16,64,512]{2,1,0:T(8,128)(2,1)} %pad_maximum_fusion.1), channel_id=1, source_target_pairs={{0,256},{16,272},{32,288},{48,304},{64,320},{80,336},{96,352},{112... | collective-permute-start | bytes 3145736 | tf_op jit(solution)/shard_map/ppermute | solution.py:27
  63.5 0.3 slice_reduce_fusion.7
  63.7 0.2 compare_reduce_fusion
  63.9 2.8 %or_and_fusion = pred[4,64,2048]{2,1,0:T(32,128)(4,1)} fusion(s32[64,2048]{1,0:T(8,128)S(1)} %broadcast_subtract_fusion, s32[4]{0:T(128)S(1)} %get-tuple-element.8, s32[4]{0:T(128)S(1)} %get-tuple-element.10, s32[4]{0:T(128)S(1)} %get-tuple-element.11, s32[4]{0:T(128)S(1)} %get-tuple-element.12, s32[4]{0:T(128)S(1)} %get-tuple-element.13, ...), kind=kLoop, calls=%fused_computation.14 | loop fusion | flops 8912896 | bytes 1187968 | tf_op jit(solution)/shard_map/and | solution.py:50
  66.7 0.0 all-gather.5.cloned.1.call-done
  66.7 1.5 copy_bitcast_fusion
  68.2 0.6 gather_fusion
  68.8 36.1 %collective-permute-done.4 = bf16[16,64,512]{2,1,0:T(8,128)(2,1)S(1)} collective-permute-done((bf16[16,64,512]{2,1,0:T(8,128)(2,1)}, bf16[16,64,512]{2,1,0:T(8,128)(2,1)S(1)}, u32[]{:S(2)}, u32[]{:S(2)}) %collective-permute-start.4) | collective-permute-done | bytes 1048608 | tf_op jit(solution)/shard_map/ppermute | solution.py:27
  104.9 0.1 broadcast_select_fusion.1
  105.0 0.2 pad_maximum_fusion
  105.2 2.1 %reshape_reshape.3 = bf16[2048,4,128]{2,1,0:T(4,128)(2,1)} reshape(bf16[32,64,512]{2,1,0:T(8,128)(2,1)S(1)} %pad_maximum_fusion) | data formatting | bytes 4194304 | tf_op jit(solution)/shard_map/reshape;reshape | solution.py:95
  107.3 1.9 %copy.32 = bf16[2048,4,128]{2,0,1:T(8,128)(2,1)S(1)} copy(bf16[2048,4,128]{2,1,0:T(4,128)(2,1)} %reshape_reshape.3) | data formatting | bytes 4194304 | tf_op jit(solution)/shard_map/reshape;reshape | solution.py:95
  109.1 2.1 %gather_fusion.6 = bf16[4,2048,128]{2,1,0:T(8,128)(2,1)} fusion(bf16[2048,4,128]{2,0,1:T(8,128)(2,1)S(1)} %copy.32, s32[1024]{0:T(1024)S(1)} %pad_clamp_fusion), kind=kCustom, calls=%fused_computation.4.clone | custom fusion | bytes 4194320 | tf_op jit(solution)/shard_map/jit(_take)/gather | solution.py:95
  111.2 47.5 %all-gather.3.cloned.1.call-done = bf16[2048,512]{1,0:T(8,128)(2,1)} async-done(((bf16[64,512]{1,0:T(8,128)(2,1)}), bf16[2048,512]{1,0:T(8,128)(2,1)}) %all-gather.3.cloned.1.call-update) | async-done | bytes 2097168 | tf_op jit(solution)/shard_map/all_gather | solution.py:103
  158.7 3.9 %copy.25 = bf16[2048,512]{0,1:T(8,128)(2,1)} copy(bf16[2048,512]{1,0:T(8,128)(2,1)} %all-gather.3.cloned.1.call-done) | data formatting | bytes 4194304 | tf_op jit(solution)/shard_map/all_gather | solution.py:103
  162.7 3.0 %copy.26 = bf16[2048,4,128]{2,0,1:T(8,128)(2,1)S(1)} copy(bf16[2048,4,128]{0,2,1:T(8,128)(2,1)} %bitcast.48) | data formatting | bytes 4194304 | tf_op jit(solution)/shard_map/reshape | solution.py:95
  165.7 2.2 %gather_fusion.2 = bf16[4,2048,128]{2,1,0:T(8,128)(2,1)} fusion(bf16[2048,4,128]{2,0,1:T(8,128)(2,1)S(1)} %copy.26, s32[1024]{0:T(1024)S(1)} %pad_clamp_fusion), kind=kCustom, calls=%fused_computation.1.clone | custom fusion | bytes 4194320 | tf_op jit(solution)/shard_map/jit(_take)/gather | solution.py:95
  167.9 0.0 copy-start.1
  167.9 2.7 %select_bitcast_fusion.1 = (bf16[2048,4,128]{2,0,1:T(8,128)(2,1)S(1)}, bf16[2048,4,128]{2,0,1:T(8,128)(2,1)S(1)}) fusion(bf16[4,2048,128]{2,1,0:T(8,128)(2,1)} %gather_fusion.2, pred[4]{0:T(512)(128)(4,1)S(1)} %iota_compare_fusion.1, bf16[4,2048,128]{2,1,0:T(8,128)(2,1)} %gather_fusion.6), kind=kLoop, calls=%fused_computation.13 | loop fusion | flops 2097152 | bytes 8388612 | tf_op jit(solution)/shard_map/jit(_take)/select_n | solution.py:95
  170.6 0.0 copy-done.1
  170.6 0.6 fusion.23
  171.3 0.7 fusion.24
  171.9 0.3 fusion.8
  172.2 0.4 convolution_bitcast_fusion
  172.6 0.3 fusion.6
  172.9 0.4 convolution_bitcast_fusion.1
  173.3 0.7 copy_bitcast_fusion.3
  (18 shorter events, 0.3 us)
Async XLA Ops:
  6.5 1.5 copy-start
  6.5 22.0 %copy-start.2 = (s32[64,8]{0,1:T(8,128)S(1)}, s32[64,8]{0,1:T(8,128)}, u32[]{:S(2)}) copy-start(s32[64,8]{0,1:T(8,128)} %param.15) | copy-start | bytes 6148
  6.5 22.1 %copy-start.3 = (s32[64,8]{0,1:T(8,128)S(1)}, s32[64,8]{0,1:T(8,128)}, u32[]{:S(2)}) copy-start(s32[64,8]{0,1:T(8,128)} %param.16) | copy-start | bytes 6148
  6.5 60.2 %all-gather.5.cloned.1.call-start = ((), (), s32[]{:S(2)}) async-start(), calls=%async_computation.1 | async-start | bytes 1114112 | tf_op jit(solution)/shard_map/all_gather | solution.py:86
  7.3 151.5 %all-gather.3.cloned.1.call-start = ((), (), s32[]{:S(2)}) async-start(), calls=%async_computation | async-start | bytes 2162688 | tf_op jit(solution)/shard_map/all_gather | solution.py:103
  10.4 6.2 %collective-permute-start = (bf16[1,64,512]{2,1,0:T(8,128)(2,1)S(1)}, bf16[1,64,512]{2,1,0:T(8,128)(2,1)S(1)}, u32[]{:S(2)}, u32[]{:S(2)}) collective-permute-start(bf16[1,64,512]{2,1,0:T(8,128)(2,1)S(1)} %broadcast_in_dim_reshape.3), channel_id=1, source_target_pairs={{0,16},{16,0},{32,48},{48,32},{64,80},{80,64},{96,112},{112,96},{1... | collective-permute-start | bytes 196616 | tf_op jit(solution)/shard_map/ppermute | solution.py:27
  16.6 8.4 %collective-permute-start.1 = (bf16[2,64,512]{2,1,0:T(8,128)(2,1)S(1)}, bf16[2,64,512]{2,1,0:T(8,128)(2,1)S(1)}, u32[]{:S(2)}, u32[]{:S(2)}) collective-permute-start(bf16[2,64,512]{2,1,0:T(8,128)(2,1)S(1)} %pad_maximum_fusion.4), channel_id=1, source_target_pairs={{0,32},{16,48},{32,0},{48,16},{64,96},{80,112},{96,64},{112,80},{1... | collective-permute-start | bytes 393224 | tf_op jit(solution)/shard_map/ppermute | solution.py:27
  25.0 8.3 %collective-permute-start.2 = (bf16[4,64,512]{2,1,0:T(8,128)(2,1)S(1)}, bf16[4,64,512]{2,1,0:T(8,128)(2,1)S(1)}, u32[]{:S(2)}, u32[]{:S(2)}) collective-permute-start(bf16[4,64,512]{2,1,0:T(8,128)(2,1)S(1)} %pad_maximum_fusion.3), channel_id=1, source_target_pairs={{0,64},{16,80},{32,96},{48,112},{64,0},{80,16},{96,32},{112,48},{1... | collective-permute-start | bytes 786440 | tf_op jit(solution)/shard_map/ppermute | solution.py:27
  33.4 21.3 %collective-permute-start.3 = (bf16[8,64,512]{2,1,0:T(8,128)(2,1)S(1)}, bf16[8,64,512]{2,1,0:T(8,128)(2,1)S(1)}, u32[]{:S(2)}, u32[]{:S(2)}) collective-permute-start(bf16[8,64,512]{2,1,0:T(8,128)(2,1)S(1)} %pad_maximum_fusion.2), channel_id=1, source_target_pairs={{0,128},{16,144},{32,160},{48,176},{64,192},{80,208},{96,224},{112... | collective-permute-start | bytes 1572872 | tf_op jit(solution)/shard_map/ppermute | solution.py:27
  55.8 49.0 %collective-permute-start.4 = (bf16[16,64,512]{2,1,0:T(8,128)(2,1)}, bf16[16,64,512]{2,1,0:T(8,128)(2,1)S(1)}, u32[]{:S(2)}, u32[]{:S(2)}) collective-permute-start(bf16[16,64,512]{2,1,0:T(8,128)(2,1)} %pad_maximum_fusion.1), channel_id=1, source_target_pairs={{0,256},{16,272},{32,288},{48,304},{64,320},{80,336},{96,352},{112... | collective-permute-start | bytes 3145736 | tf_op jit(solution)/shard_map/ppermute | solution.py:27
  167.9 2.7 %copy-start.1 = (pred[4,64,2048]{2,1,0:T(32,128)(4,1)S(1)}, pred[4,64,2048]{2,1,0:T(32,128)(4,1)}, u32[]{:S(2)}) copy-start(pred[4,64,2048]{2,1,0:T(32,128)(4,1)} %or_and_fusion) | copy-start | bytes 1572868
Sparse Core Ops, SparseCore 0:
  9.5 46.5 all-gather.4
  59.2 99.4 all-gather.2
